TPU v7x, 32 devices: a whole 2x2x4 slice. The times are simulated.
32 devices in a mesh: dp: 2 (over core), seq: 16 (over z, y, x).
Axes of the slice: x: 2, y: 2, z: 4, core: 2. Of those that a mesh axis runs over, the one named last changes fastest.
Arguments:
- inputs: bfloat16 [2, 8192, 768], P('dp', 'seq'), may hold values from -6 to 6
- cotangent: bfloat16 [2, 8192, 768], P('dp', 'seq'), may hold values from -1.5 to 1.5
- factor_one: bfloat16 [16, 512, 512], P('seq'), may hold values from -0.25 to 0.25
- factor_two: bfloat16 [512, 16, 16], P('seq'), may hold values from -1.5 to 1.5
- up_weight: bfloat16 [2, 384, 1536], P(None, None, 'dp'), may hold values from -0.3125 to 0.3125
- down_weight: bfloat16 [2, 1536, 384], P(None, 'dp'), may hold values from -0.15625 to 0.15625
Outputs:
- outputs: bfloat16 [2, 8192, 768], P('dp', 'seq')
- grad_inputs: bfloat16 [2, 8192, 768], P('dp', 'seq')
- grad_factor_one: float32 [16, 512, 512], P('seq', 'dp')
- grad_factor_two: float32 [512, 16, 16], P('seq', 'dp')
All inputs are finite; a program needn't handle non-finite values.
Results may differ from a plain program's by a relative error of at most 0.0066.
Values may be sent and summed in bfloat16 or wider, within the bound.
A program may use at most 64 MiB of HBM per device.

v0:
```python
import jax
import jax.numpy as jnp
from jax import lax
from jax.sharding import PartitionSpec as P


def shards(inputs, cotangent, factor_one, factor_two, up_weight, down_weight):
    rows = factor_one.shape[0]
    block = factor_one.shape[1]
    channels = inputs.shape[2]
    groups = up_weight.shape[0]
    group_ch = up_weight.shape[1]
    tok_rows = rows * block
    mixed_one = jnp.einsum(
        "apb,abc->apc", factor_one, inputs, preferred_element_type=jnp.float32
    ).astype(jnp.bfloat16)
    cols_one = lax.all_to_all(mixed_one, "seq", split_axis=1, concat_axis=0, tiled=True)
    mixed = jnp.einsum(
        "pqa,apc->qpc", factor_two, cols_one, preferred_element_type=jnp.float32
    ).astype(jnp.bfloat16)
    mixed_cols, cols_one = (mixed, cols_one)
    mixed_two = lax.all_to_all(mixed_cols, "seq", split_axis=0, concat_axis=1, tiled=True)
    mixed_f = mixed_two.reshape(tok_rows, channels).astype(jnp.float32)
    input_f = inputs.reshape(tok_rows, channels).astype(jnp.float32)
    silu_vals, silu_back = jax.vjp(jax.nn.silu, input_f)
    gated = (mixed_f * silu_vals).astype(jnp.bfloat16)
    gated_rows = gated.reshape(tok_rows, groups, group_ch)
    up_full, down_full = (
        lax.all_gather(up_weight, "dp", axis=2, tiled=True),
        lax.all_gather(down_weight, "dp", axis=1, tiled=True),
    )
    pre = jnp.einsum("tnc,nch->tnh", gated_rows, up_full, preferred_element_type=jnp.float32)
    hidden_act, gelu_back = jax.vjp(jax.nn.gelu, pre)
    hidden = hidden_act.astype(jnp.bfloat16)
    result = gated_rows.astype(jnp.float32) + jnp.einsum(
        "tnh,nhc->tnc", hidden, down_full, preferred_element_type=jnp.float32
    )
    outputs = result.reshape(1, tok_rows, channels).astype(jnp.bfloat16)
    up_back, down_back = (
        lax.all_gather(up_weight, "dp", axis=2, tiled=True),
        lax.all_gather(down_weight, "dp", axis=1, tiled=True),
    )
    cot_rows = cotangent.reshape(tok_rows, groups, group_ch)
    grad_hidden = jnp.einsum(
        "tnc,nhc->tnh", cot_rows, down_back, preferred_element_type=jnp.float32
    )
    grad_pre = gelu_back(grad_hidden)[0].astype(jnp.bfloat16)
    grad_gated = cot_rows.astype(jnp.float32) + jnp.einsum(
        "tnh,nch->tnc", grad_pre, up_back, preferred_element_type=jnp.float32
    )
    grad_gated = grad_gated.reshape(tok_rows, channels)
    grad_two = (grad_gated * silu_vals).astype(jnp.bfloat16).reshape(rows, block, channels)
    grad_gate_in = silu_back(grad_gated * mixed_f)[0]
    grad_cols = lax.all_to_all(grad_two, "seq", split_axis=1, concat_axis=0, tiled=True)
    grad_one = jnp.einsum(
        "pqa,qpc->apc", factor_two, grad_cols, preferred_element_type=jnp.float32
    ).astype(jnp.bfloat16)
    grad_one_cols, grad_cols = (grad_one, grad_cols)
    term_two = jnp.einsum("qpc,apc->pqa", grad_cols, cols_one, preferred_element_type=jnp.float32)
    grad_one = lax.all_to_all(grad_one_cols, "seq", split_axis=0, concat_axis=1, tiled=True)
    term_one = jnp.einsum("apc,abc->apb", grad_one, inputs, preferred_element_type=jnp.float32)
    grad_in = grad_gate_in.reshape(rows, block, channels) + jnp.einsum(
        "apb,apc->abc", factor_one, grad_one, preferred_element_type=jnp.float32
    )
    grad_inputs = grad_in.astype(jnp.bfloat16)
    grad_first, grad_second = (
        lax.psum_scatter(term_one, "dp", scatter_dimension=1, tiled=True),
        lax.psum_scatter(term_two, "dp", scatter_dimension=1, tiled=True),
    )
    return (outputs, grad_inputs, grad_first, grad_second)


def solution(mesh):
    in_specs = (
        P("dp", "seq", None),
        P("dp", "seq", None),
        P("seq", None, None),
        P("seq", None, None),
        P(None, None, "dp"),
        P(None, "dp", None),
    )
    out_specs = (
        P("dp", "seq", None),
        P("dp", "seq", None),
        P("seq", "dp", None),
        P("seq", "dp", None),
    )
    return jax.shard_map(shards, mesh=mesh, in_specs=in_specs, out_specs=out_specs, check_vma=False)
```

profile of v0, /device:TPU:0, one launch (start us, length us, event | category | flops | bytes accessed | tf_op | source)
XLA Modules:
  0.0 196.8 jit_solution(8986361935761234434)
XLA Ops:
  7.2 0.7 all-gather.3.cloned.1.call-update
  7.9 0.3 copy-done
  8.2 1.7 fusion.26
  9.9 1.2 copy.139
  11.1 0.5 broadcast.59
  11.7 5.4 %reduce = bf16[512,768]{1,0:T(8,128)(2,1)S(1)} reduce(bf16[512,1,768]{2,1,0:T(2,128)(2,1)S(1)} %bitcast.106, bf16[]{:T(256)} %broadcast.59), dimensions={1}, to_apply=%bitcast.105.reduce_sub_computation | reduce | bytes 1572866
  17.1 1.1 reshape.87
  18.2 8.4 %all-to-all-start = ((bf16[16,2,12288]{2,1,0:T(2,128)(2,1)}), bf16[16,2,12288]{2,1,0:T(2,128)(2,1)S(1)}, u32[]{:S(2)}, u32[]{:S(2)}) async-start(bf16[16,2,12288]{2,1,0:T(2,128)(2,1)} %reshape.87), calls=%async_computation | async-start | bytes 1572864 | tf_op jit(solution)/shard_map/all_to_all | solution.py:17
  26.7 1.4 copy.104
  28.2 0.2 copy.113
  28.4 18.0 %all-to-all-done = bf16[16,2,12288]{2,1,0:T(2,128)(2,1)S(1)} async-done(((bf16[16,2,12288]{2,1,0:T(2,128)(2,1)}), bf16[16,2,12288]{2,1,0:T(2,128)(2,1)S(1)}, u32[]{:S(2)}, u32[]{:S(2)}) %all-to-all-start) | async-done | bytes 786464 | tf_op jit(solution)/shard_map/all_to_all | solution.py:17
  46.4 0.7 reshape.88
  47.1 0.1 copy.126
  47.2 0.9 copy-done.3
  48.2 0.6 fusion.24
  48.8 1.1 copy.99
  49.9 5.0 %all-to-all-start.1 = ((bf16[16,32,768]{2,1,0:T(8,128)(2,1)}), bf16[16,32,768]{2,1,0:T(8,128)(2,1)S(1)}, u32[]{:S(2)}, u32[]{:S(2)}) async-start(bf16[16,32,768]{2,1,0:T(8,128)(2,1)} %copy.99), calls=%async_computation.1 | async-start | bytes 1572864 | tf_op jit(solution)/shard_map/all_to_all | solution.py:22
  54.9 1.4 copy.125
  56.4 1.2 copy.105
  57.6 16.0 %all-to-all-done.1 = bf16[16,32,768]{2,1,0:T(8,128)(2,1)S(1)} async-done(((bf16[16,32,768]{2,1,0:T(8,128)(2,1)}), bf16[16,32,768]{2,1,0:T(8,128)(2,1)S(1)}, u32[]{:S(2)}, u32[]{:S(2)}) %all-to-all-start.1) | async-done | bytes 786464 | tf_op jit(solution)/shard_map/all_to_all | solution.py:22
  73.6 2.0 %reshape.84 = f32[512,2,384]{2,1,0:T(2,128)} reshape(bf16[16,32,768]{2,1,0:T(8,128)(2,1)S(1)} %all-to-all-done.1) | data formatting | bytes 2359296 | tf_op jit(solution)/shard_map/convert_element_type | solution.py:23
  75.6 3.7 %copy.102 = f32[512,2,384]{0,2,1:T(8,128)} copy(f32[512,2,384]{2,1,0:T(2,128)} %reshape.84) | data formatting | bytes 3145728 | tf_op jit(solution)/shard_map/convert_element_type | solution.py:23
  79.3 2.4 %multiply_convert_fusion.1 = bf16[512,2,384]{0,2,1:T(8,128)(2,1)S(1)} fusion(f32[512,2,384]{0,2,1:T(8,128)} %copy.102, f32[512,2,384]{0,2,1:T(8,128)} %bitcast.111), kind=kLoop, calls=%fused_computation.33 | loop fusion | flops 2359296 | bytes 3932160 | tf_op jit(solution)/shard_map/convert_element_type | solution.py:26
  81.7 6.4 %fusion.47 = f32[2,512,1536]{2,1,0:T(8,128)} fusion(bf16[512,2,384]{0,2,1:T(8,128)(2,1)S(1)} %multiply_convert_fusion.1, bf16[2,384,1536]{2,1,0:T(8,128)(2,1)} %all-gather.3.cloned.1.call-done), kind=kOutput, calls=%fused_computation.63 | convolution fusion | flops 1207959552 | bytes 9437184 | tf_op jit(solution)/shard_map/tnc,nch->tnh/dot_general | solution.py:32
  88.1 11.6 %bitcast_add_fusion = f32[512,2,384]{0,2,1:T(8,128)} fusion(bf16[512,2,384]{0,2,1:T(8,128)(2,1)} %bitcast.119, bf16[2,384,1536]{2,1,0:T(8,128)(2,1)} %all-gather.3.cloned.1.call-done, f32[2,512,1536]{2,1,0:T(8,128)} %fusion.47, bf16[2,1536,384]{1,2,0:T(8,128)(2,1)} %all-gather.5.cloned.1.call-done), kind=kOutput, calls=%fused_computation.29 | convolution fusion | flops 2448162816 | bytes 13369344 | tf_op jit(solution)/shard_map/tnh,nch->tnc/dot_general | solution.py:48
  99.7 3.1 %copy.124 = f32[1,512,768]{2,1,0:T(8,128)} copy(f32[1,512,768]{1,2,0:T(8,128)} %bitcast.118) | data formatting | bytes 3145728 | tf_op jit(solution)/shard_map/reshape | solution.py:51
  102.7 1.9 multiply_convert_fusion
  104.6 2.4 %copy.138 = bf16[1,512,768]{2,0,1:T(2,128)(2,1)} copy(bf16[1,512,768]{2,1,0:T(8,128)(2,1)S(1)} %multiply_convert_fusion) | data formatting | bytes 1572864 | tf_op jit(solution)/shard_map/convert_element_type | solution.py:52
  107.0 6.6 %reduce.1 = bf16[512,768]{1,0:T(8,128)(2,1)S(1)} reduce(bf16[512,1,768]{2,1,0:T(2,128)(2,1)} %bitcast.107, bf16[]{:T(256)} %broadcast.59), dimensions={1}, to_apply=%bitcast.104.reduce_sub_computation | reduce | bytes 1572866
  113.7 1.1 reshape.89
  114.7 25.1 %all_to_all.42 = bf16[16,2,12288]{2,1,0:T(2,128)(2,1)S(1)} all-to-all(bf16[16,2,12288]{2,1,0:T(2,128)(2,1)} %reshape.89), channel_id=1, replica_groups=mesh['dp'=2,'seq'=16] {'seq'}, dimensions={0} | all-to-all | bytes 1572864 | tf_op jit(solution)/shard_map/all_to_all | solution.py:54
  139.8 2.1 %reshape.90 = bf16[512,1,768]{2,1,0:T(2,128)(2,1)} reshape(bf16[16,2,12288]{2,1,0:T(2,128)(2,1)S(1)} %all_to_all.42) | data formatting | bytes 1572864
  141.9 1.5 copy.127
  143.4 1.0 copy-done.4
  144.4 0.6 fusion.25
  145.0 1.1 copy.114
  146.1 3.6 %all-to-all-start.3 = ((bf16[16,32,768]{2,1,0:T(8,128)(2,1)}), bf16[16,32,768]{2,1,0:T(8,128)(2,1)S(1)}, u32[]{:S(2)}, u32[]{:S(2)}) async-start(bf16[16,32,768]{2,1,0:T(8,128)(2,1)} %copy.114), calls=%async_computation.3 | async-start | bytes 1572864 | tf_op jit(solution)/shard_map/all_to_all | solution.py:60
  149.7 3.0 %fusion.30 = f32[32,16,16]{2,1,0:T(8,128)} fusion(bf16[16,32,768]{2,1,0:T(8,128)(2,1)} %bitcast.117, bf16[16,32,768]{2,1,0:T(8,128)(2,1)} %bitcast.115), kind=kOutput, calls=%fused_computation.44 | convolution fusion | flops 12582912 | bytes 1605632 | tf_op jit(solution)/shard_map/qpc,apc->pqa/dot_general | solution.py:59
  152.8 15.3 %all-to-all-done.3 = bf16[16,32,768]{2,1,0:T(8,128)(2,1)S(1)} async-done(((bf16[16,32,768]{2,1,0:T(8,128)(2,1)}), bf16[16,32,768]{2,1,0:T(8,128)(2,1)S(1)}, u32[]{:S(2)}, u32[]{:S(2)}) %all-to-all-start.3) | async-done | bytes 786464 | tf_op jit(solution)/shard_map/all_to_all | solution.py:60
  168.2 1.6 convolution_bitcast_fusion
  169.8 1.2 copy.95
  171.0 6.2 %fusion.21 = bf16[512,2,384]{0,2,1:T(8,128)(2,1)S(1)} fusion(bf16[512,2,384]{0,2,1:T(8,128)(2,1)} %copy-done.2, bf16[2,1536,384]{1,2,0:T(8,128)(2,1)} %all-gather.5.cloned.1.call-done, f32[2,512,1536]{2,1,0:T(8,128)} %fusion.47), kind=kOutput, calls=%fused_computation.31 | convolution fusion | flops 1223294976 | bytes 10223616 | tf_op jit(solution)/shard_map/tnh,nhc->tnc/dot_general | solution.py:35
  177.2 1.2 copy.117
  178.3 1.3 convert_element_type.106
  179.6 3.2 %copy.109 = f32[512,768]{0,1:T(8,128)} copy(f32[512,768]{1,0:T(8,128)} %bitcast.110) | data formatting | bytes 3145728 | tf_op jit(solution)/shard_map/convert_element_type | solution.py:23
  182.8 1.6 copy.119
  184.4 3.6 %fusion.27 = bf16[1,512,768]{1,2,0:T(8,128)(2,1)} fusion(bf16[512,768]{1,0:T(8,128)(2,1)S(1)} %bitcast.113, f32[512,768]{0,1:T(8,128)} %copy.109, f32[512,2,384]{0,2,1:T(8,128)S(1)} %copy-done.5, bf16[1,512,768]{1,2,0:T(8,128)(2,1)} %copy.95, bf16[1,512,512]{2,1,0:T(8,128)(2,1)S(1)} %copy-done), kind=kOutput, calls=%fused_computation.41 | convolution fusion | flops 407764992 | bytes 6029312 | tf_op jit(solution)/shard_map/apb,apc->abc/dot_general | solution.py:62
  188.0 2.3 %copy.118 = bf16[1,512,768]{2,1,0:T(8,128)(2,1)} copy(bf16[1,512,768]{1,2,0:T(8,128)(2,1)} %fusion.27) | data formatting | bytes 1572864
  (26 shorter events, 0.3 us)
Async XLA Ops:
  7.2 1.0 copy-start
  7.2 74.5 %all-gather.3.cloned.1.call-start = ((), (), s32[]{:S(2)}) async-start(), calls=%async_computation.6 | async-start | bytes 3538944 | tf_op jit(solution)/shard_map/all_gather | solution.py:29
  17.1 9.6 %copy-start.6 = (bf16[2,768,384]{2,1,0:T(8,128)(2,1)S(1)}, bf16[2,768,384]{2,1,0:T(8,128)(2,1)}, u32[]{:S(2)}) copy-start(bf16[2,768,384]{2,1,0:T(8,128)(2,1)} %param.11) | copy-start | bytes 3538948
  18.2 10.0 %copy-start.8 = (bf16[32,16,16]{0,2,1:T(8,128)(2,1)S(1)}, bf16[32,16,16]{0,2,1:T(8,128)(2,1)}, u32[]{:S(2)}) copy-start(bf16[32,16,16]{0,2,1:T(8,128)(2,1)} %param.9) | copy-start | bytes 49156
  18.2 28.2 %all-to-all-start = ((bf16[16,2,12288]{2,1,0:T(2,128)(2,1)}), bf16[16,2,12288]{2,1,0:T(2,128)(2,1)S(1)}, u32[]{:S(2)}, u32[]{:S(2)}) async-start(bf16[16,2,12288]{2,1,0:T(2,128)(2,1)} %reshape.87), calls=%async_computation | async-start | bytes 1572864 | tf_op jit(solution)/shard_map/all_to_all | solution.py:17
  26.6 61.5 %all-gather.5.cloned.1.call-start = ((), (), s32[]{:S(2)}) async-start(), calls=%async_computation.7 | async-start | bytes 3538944 | tf_op jit(solution)/shard_map/all_gather | solution.py:30
  47.2 1.0 copy-start.3
  48.2 6.7 %copy-start.1 = (bf16[1,512,768]{2,1,0:T(8,128)(2,1)S(1)}, bf16[1,512,768]{2,1,0:T(8,128)(2,1)}, u32[]{:S(2)}) copy-start(bf16[1,512,768]{2,1,0:T(8,128)(2,1)} %param.6) | copy-start | bytes 2359300
  49.9 6.5 %copy-start.7 = (bf16[1,512,768]{2,1,0:T(8,128)(2,1)S(1)}, bf16[1,512,768]{2,1,0:T(8,128)(2,1)}, u32[]{:S(2)}) copy-start(bf16[1,512,768]{2,1,0:T(8,128)(2,1)} %param.7) | copy-start | bytes 2359300
  49.9 23.7 %all-to-all-start.1 = ((bf16[16,32,768]{2,1,0:T(8,128)(2,1)}), bf16[16,32,768]{2,1,0:T(8,128)(2,1)S(1)}, u32[]{:S(2)}, u32[]{:S(2)}) async-start(bf16[16,32,768]{2,1,0:T(8,128)(2,1)} %copy.99), calls=%async_computation.1 | async-start | bytes 1572864 | tf_op jit(solution)/shard_map/all_to_all | solution.py:22
  81.6 6.5 %copy-start.2 = (bf16[512,2,384]{0,2,1:T(8,128)(2,1)}, bf16[512,2,384]{0,2,1:T(8,128)(2,1)S(1)}, u32[]{:S(2)}) copy-start(bf16[512,2,384]{0,2,1:T(8,128)(2,1)S(1)} %multiply_convert_fusion.1) | copy-start | bytes 2359300
  143.4 1.0 copy-start.4
  146.1 22.1 %all-to-all-start.3 = ((bf16[16,32,768]{2,1,0:T(8,128)(2,1)}), bf16[16,32,768]{2,1,0:T(8,128)(2,1)S(1)}, u32[]{:S(2)}, u32[]{:S(2)}) async-start(bf16[16,32,768]{2,1,0:T(8,128)(2,1)} %copy.114), calls=%async_computation.3 | async-start | bytes 1572864 | tf_op jit(solution)/shard_map/all_to_all | solution.py:60
  149.7 33.1 %reduce-scatter.5.cloned.1.call-start = ((), (), s32[]{:S(2)}) async-start(), calls=%async_computation.9 | async-start | bytes 393216 | tf_op jit(solution)/shard_map/reduce_scatter | solution.py:68
  152.8 37.5 %reduce-scatter.3.cloned.1.call-start = ((), (), s32[]{:S(2)}) async-start(), calls=%async_computation.8 | async-start | bytes 1572864 | tf_op jit(solution)/shard_map/reduce_scatter | solution.py:67
  179.6 4.8 %copy-start.5 = (f32[512,2,384]{0,2,1:T(8,128)S(1)}, f32[512,2,384]{0,2,1:T(8,128)}, u32[]{:S(2)}) copy-start(f32[512,2,384]{0,2,1:T(8,128)} %bitcast_add_fusion) | copy-start | bytes 4718596
Sparse Core Ops, SparseCore 0:
  9.6 13.6 all-gather.2
  29.0 12.2 all-gather.4
  152.9 8.9 reduce-scatter.4
  170.0 7.6 reduce-scatter.2
where the time goes:
time: 198 us; the launch traced here: 197 us
  waiting for transfers between devices  50.1 us (25%)
  local copies, waits for them, and re-layouts  37.6 us (19%)
  matrix products  35.2 us (18%)
  blocking collectives  25.1 us (13%)
  other arithmetic  17.6 us (9%)
  starting transfers between devices  17.2 us (9%)
  between operations  14 us (7%)
    all_to_all x1, blocking collectives, shards(): lax.all_to_all(grad_two, 'seq', split_axis=1, concat_axis=0, tiled=True)  25.1 us
    unnamed x32, local copies, waits for them, and re-layouts  18.4 us
    all_to_all x1, waiting for transfers between devices, shards(): lax.all_to_all(mixed_one, 'seq', split_axis=1, concat_axis=0, tiled=True)  18 us
    all_to_all x1, waiting for transfers between devices, shards(): lax.all_to_all(mixed_cols, 'seq', split_axis=0, concat_axis=1, tiled=True)  16 us
    all_to_all x1, waiting for transfers between devices, shards(): lax.all_to_all(grad_one_cols, 'seq', split_axis=0, concat_axis=1, tiled=T...  15.3 us
    unnamed x2, other arithmetic  12 us
    dot_general x1, matrix products, shards(): jnp.einsum('tnh,nch->tnc', grad_pre, up_back, preferred_element_type=jnp....  11.6 us
    convert_element_type x3, local copies, waits for them, and re-layouts, shards(): mixed_f = mixed_two.reshape(tok_rows, channels).astype(jnp.float32)  8.84 us
  transfers between devices with their start and end apart: 7, of which 3 were waited for; matrix products, arithmetic and copies ran while one was open for 29% of the time, Pallas kernels for 0%

commit v1 on v0

v1 whole, which is shorter than its diff:
```python
import functools

import jax
import jax.numpy as jnp
from jax import lax
from jax.experimental import pallas as pl
from jax.experimental.pallas import tpu as pltpu
from jax.sharding import PartitionSpec as P

MESH = pl.DeviceIdType.MESH
F32 = jnp.float32
BF16 = jnp.bfloat16
GELU_A = 0.7978845608028654
GELU_B = 0.044715
TOK_TILE = 128
ROW_TILE = 256


def dot(a, b):
    return jnp.dot(a, b, preferred_element_type=F32)


def dot_nt(a, b):
    return lax.dot_general(a, b, (((1,), (1,)), ((), ())), preferred_element_type=F32)


def kernel(
    n_seq, n_dp,
    x_ref, cot_ref, f1_ref, f2_ref, up_ref, down_ref,
    out_ref, gin_ref, g1_ref, g2_ref,
    src, dst, up_all, down_all, mix, mix_t, f1_t, sel, perm, gate, t1, t1_in, t2, t2_in,
    send_sem, recv_sem, w_send, w_recv, w_local, r_send, r_recv,
):
    me = lax.axis_index("seq")
    core = lax.axis_index("dp")
    block, channels = x_ref.shape
    groups, _, parts, width = src.shape[1], src.shape[2], src.shape[3], src.shape[4]
    rows_one = t1_in.shape[1]
    rows_two = t2_in.shape[1]

    barrier = pltpu.get_barrier_semaphore()

    def greet_seq(k, carry):
        pl.semaphore_signal(
            barrier, inc=1, device_id={"seq": lax.rem(me + k, n_seq)}, device_id_type=MESH
        )
        return carry

    def greet_dp(k, carry):
        pl.semaphore_signal(
            barrier, inc=1, device_id={"dp": lax.rem(core + k, n_dp)}, device_id_type=MESH
        )
        return carry

    lax.fori_loop(1, n_seq, greet_seq, 0)
    lax.fori_loop(1, n_dp, greet_dp, 0)

    def cols(g):
        return pl.ds(g * width, width)

    def flat(ref, phase, g):
        return ref[phase, g].reshape(block, width)

    def send(phase, g):
        def one(k, carry):
            peer = lax.rem(me + k, n_seq)
            pltpu.make_async_remote_copy(
                src_ref=src.at[phase, g, peer],
                dst_ref=dst.at[phase, g, me],
                send_sem=send_sem.at[phase, g],
                recv_sem=recv_sem.at[phase, g],
                device_id={"seq": peer},
                device_id_type=MESH,
            ).start()
            return carry

        lax.fori_loop(1, n_seq, one, 0)
        dst[phase, g, me] = src[phase, g, me]

    def receive(phase, g):
        span = dst.at[phase, g, pl.ds(0, n_seq - 1)]
        pltpu.make_async_copy(span, span, recv_sem.at[phase, g]).wait()

    def row_loop(total, tile, body):
        def step(i, carry):
            body(pl.ds(pl.multiple_of(i * tile, tile), tile))
            return carry

        lax.fori_loop(0, total // tile, step, 0)

    seq_tile = max(1, ROW_TILE // parts)

    def mul_into(phase, g, left, right):
        def step(i, carry):
            tile = seq_tile * parts
            rows = pl.ds(pl.multiple_of(i * tile, tile), tile)
            value = dot(left[rows, :], right()).astype(BF16)
            src[phase, g, pl.ds(i * seq_tile, seq_tile)] = value.reshape(seq_tile, parts, width)
            return carry

        lax.fori_loop(0, n_seq // seq_tile, step, 0)

    mul_into(0, 0, f1_ref, lambda: x_ref[:, cols(0)])
    pl.semaphore_wait(barrier, n_seq + n_dp - 2)
    send(0, 0)

    def send_weights(k, carry):
        peer = lax.rem(core + k, n_dp)
        for i, (mine, everyone) in enumerate(((up_ref, up_all), (down_ref, down_all))):
            pltpu.make_async_remote_copy(
                src_ref=mine,
                dst_ref=everyone.at[core],
                send_sem=w_send.at[i],
                recv_sem=w_recv.at[i],
                device_id={"dp": peer},
                device_id_type=MESH,
            ).start()
        return carry

    lax.fori_loop(1, n_dp, send_weights, 0)
    own = [
        pltpu.make_async_copy(up_ref, up_all.at[core], w_local.at[0]),
        pltpu.make_async_copy(down_ref, down_all.at[core], w_local.at[1]),
    ]
    for copy in own:
        copy.start()
    for g in range(1, groups):
        mul_into(0, g, f1_ref, lambda: x_ref[:, cols(g)])
        send(0, g)

    def iota(shape, axis):
        return lax.broadcasted_iota(jnp.int32, shape, axis)

    square = (block, block)
    per = n_seq // n_dp
    a_row, a_col = iota((n_seq, block), 0), iota((n_seq, block), 1)
    spread = jnp.where(a_row == a_col // parts, 1.0, 0.0).astype(BF16)
    k_row, k_col = iota((block, 128), 0), iota((block, 128), 1)
    sel[...] = jnp.where(k_row // parts == k_col, 1.0, 0.0).astype(BF16)
    row, col = iota(square, 0), iota(square, 1)
    to_q = (row // (parts * per)) * per + row % per
    to_p = (row // per) % parts
    perm[...] = jnp.where(col == to_q * parts + to_p, 1.0, 0.0).astype(BF16)
    order = jnp.where(col == (row % parts) * n_seq + row // parts, 1.0, 0.0).astype(BF16)
    wide = dot(f2_ref[...], spread).astype(BF16)
    full = dot(order, wide)
    full = jnp.where(row % parts == col % parts, full, 0.0)
    mix[...] = full.astype(BF16)
    mix_t[...] = full.T.astype(BF16)
    f1_t[...] = f1_ref[...].astype(F32).T.astype(BF16)

    for g in range(groups):
        receive(0, g)
        mul_into(1, g, mix, lambda: flat(dst, 0, g))
        send(1, g)

    for copy in own:
        copy.wait()
    for i, everyone in enumerate((up_all, down_all)):
        span = everyone.at[pl.ds(0, n_dp - 1)]
        pltpu.make_async_copy(span, span, w_recv.at[i]).wait()

    tok_seq = max(1, TOK_TILE // parts)

    def mlp(g):
        def step(i, carry):
            tile = tok_seq * parts
            rows = pl.ds(pl.multiple_of(i * tile, tile), tile)
            blocks = pl.ds(i * tok_seq, tok_seq)
            x = x_ref[rows, cols(g)].astype(F32)
            sig = 1.0 / (1.0 + jnp.exp(-x))
            silu = x * sig
            mixed = dst[1, g, blocks].reshape(tile, width).astype(F32)
            gated = (mixed * silu).astype(BF16)
            cot = cot_ref[rows, cols(g)]
            result = gated.astype(F32)
            back = cot.astype(F32)
            for d in range(n_dp):
                up, down = up_all[d, g], down_all[d, g]
                pre = dot(gated, up)
                grad_hidden = dot_nt(cot, down)
                sq = pre * pre
                th = jnp.tanh(pre * (GELU_A + (GELU_A * GELU_B) * sq))
                half = 0.5 + 0.5 * th
                hidden = (pre * half).astype(BF16)
                slope = half + (pre * half) * (1.0 - th) * (
                    GELU_A + (3.0 * GELU_A * GELU_B) * sq
                )
                grad_pre = (grad_hidden * slope).astype(BF16)
                result += dot(hidden, down)
                back += dot_nt(grad_pre, up)
            out_ref[rows, cols(g)] = result.astype(BF16)
            src[2, g, blocks] = (back * silu).astype(BF16).reshape(tok_seq, parts, width)
            gate[rows, cols(g)] = back * mixed * (sig * (1.0 + x * (1.0 - sig)))
            return carry

        lax.fori_loop(0, n_seq // tok_seq, step, 0)

    for g in range(groups):
        receive(1, g)
        mlp(g)
        send(2, g)

    for g in range(groups):
        receive(2, g)
        mul_into(3, g, mix_t, lambda: flat(dst, 2, g))
        send(3, g)

    def term_two(rows):
        total = None
        for g in range(groups):
            grads = dot(perm[rows, :], flat(dst, 2, g)).astype(BF16)
            part = dot_nt(grads, flat(dst, 0, g))
            total = part if total is None else total + part
        start = rows.start
        r = start + iota(total.shape, 0)
        c = iota(total.shape, 1)
        total = jnp.where((r // per) % parts == c % parts, total, 0.0)
        high = total.astype(BF16)
        rest = total - high.astype(F32)
        low = rest.astype(BF16)
        last = (rest - low.astype(F32)).astype(BF16)
        t2[rows, :] = dot(high, sel[...]) + dot(low, sel[...]) + dot(last, sel[...])

    row_loop(block, ROW_TILE, term_two)

    def reduce_start(which, whole, landed, size):
        def one(k, carry):
            peer = lax.rem(core + k, n_dp)
            pltpu.make_async_remote_copy(
                src_ref=whole.at[pl.ds(pl.multiple_of(peer * size, size), size)],
                dst_ref=landed.at[core],
                send_sem=r_send.at[which],
                recv_sem=r_recv.at[which],
                device_id={"dp": peer},
                device_id_type=MESH,
            ).start()
            return carry

        lax.fori_loop(1, n_dp, one, 0)
        landed[core] = whole[pl.ds(pl.multiple_of(core * size, size), size), :]

    def reduce_end(which, whole, landed, size, out):
        span = landed.at[pl.ds(0, n_dp - 1)]
        pltpu.make_async_copy(span, span, r_recv.at[which]).wait()
        total = landed[0]
        for d in range(1, n_dp):
            total += landed[d]
        out[...] = total
        sent = whole.at[pl.ds(0, (n_dp - 1) * size)]
        pltpu.make_async_copy(sent, sent, r_send.at[which]).wait()

    reduce_start(1, t2, t2_in, rows_two)

    for g in range(groups):
        receive(3, g)
        grads = flat(dst, 3, g)
        seqs = x_ref[:, cols(g)]
        if g == 0:
            t1[...] = dot_nt(grads, seqs)
        else:
            t1[...] += dot_nt(grads, seqs)
        if g == groups - 1:
            reduce_start(0, t1, t1_in, rows_one)
        gin_ref[:, cols(g)] = (gate[:, cols(g)] + dot(f1_t[...], grads)).astype(BF16)

    reduce_end(1, t2, t2_in, rows_two, g2_ref)
    reduce_end(0, t1, t1_in, rows_one, g1_ref)
    for i, everyone in enumerate((up_all, down_all)):
        span = everyone.at[pl.ds(0, n_dp - 1)]
        pltpu.make_async_copy(span, span, w_send.at[i]).wait()
    for phase in range(4):
        for g in range(groups):
            span = src.at[phase, g, pl.ds(0, n_seq - 1)]
            pltpu.make_async_copy(span, span, send_sem.at[phase, g]).wait()


def shards(n_seq, n_dp, inputs, cotangent, factor_one, factor_two, up_weight, down_weight):
    _, block, channels = inputs.shape
    groups, width, hid = up_weight.shape
    parts = block // n_seq
    per = n_seq // n_dp
    vmem = pl.BlockSpec(memory_space=pltpu.VMEM)
    anywhere = pl.BlockSpec(memory_space=pl.ANY)
    rows_one, rows_two = block // n_dp, parts * per
    exchange = pltpu.VMEM((4, groups, n_seq, parts, width), BF16)
    flops = 2 * block * block * channels * 6 + 2 * block * width * hid * n_dp * groups * 4
    out, gin, g1, g2 = pl.pallas_call(
        functools.partial(kernel, n_seq, n_dp),
        out_shape=(
            jax.ShapeDtypeStruct((block, channels), BF16),
            jax.ShapeDtypeStruct((block, channels), BF16),
            jax.ShapeDtypeStruct((rows_one, block), F32),
            jax.ShapeDtypeStruct((rows_two, 128), F32),
        ),
        in_specs=[vmem, vmem, vmem, vmem, anywhere, anywhere],
        out_specs=(vmem, vmem, vmem, vmem),
        scratch_shapes=[
            exchange,
            exchange,
            pltpu.VMEM((n_dp, groups, width, hid), BF16),
            pltpu.VMEM((n_dp, groups, hid, width), BF16),
            pltpu.VMEM((block, block), BF16),
            pltpu.VMEM((block, block), BF16),
            pltpu.VMEM((block, block), BF16),
            pltpu.VMEM((block, 128), BF16),
            pltpu.VMEM((block, block), BF16),
            pltpu.VMEM((block, channels), F32),
            pltpu.VMEM((block, block), F32),
            pltpu.VMEM((n_dp, rows_one, block), F32),
            pltpu.VMEM((block, 128), F32),
            pltpu.VMEM((n_dp, rows_two, 128), F32),
            pltpu.SemaphoreType.DMA((4, groups)),
            pltpu.SemaphoreType.DMA((4, groups)),
            pltpu.SemaphoreType.DMA((2,)),
            pltpu.SemaphoreType.DMA((2,)),
            pltpu.SemaphoreType.DMA((2,)),
            pltpu.SemaphoreType.DMA((2,)),
            pltpu.SemaphoreType.DMA((2,)),
        ],
        compiler_params=pltpu.CompilerParams(
            collective_id=0, has_side_effects=True, vmem_limit_bytes=52 * 2**20
        ),
        cost_estimate=pl.CostEstimate(flops=flops, bytes_accessed=2**23, transcendentals=2**21),
    )(
        inputs[0], cotangent[0], factor_one[0],
        factor_two.reshape(block, n_seq), up_weight, down_weight,
    )
    return out[None], gin[None], g1[None], g2[:, :n_seq].reshape(parts, per, n_seq)


def solution(mesh):
    in_specs = (
        P("dp", "seq", None),
        P("dp", "seq", None),
        P("seq", None, None),
        P("seq", None, None),
        P(None, None, "dp"),
        P(None, "dp", None),
    )
    out_specs = (
        P("dp", "seq", None),
        P("dp", "seq", None),
        P("seq", "dp", None),
        P("seq", "dp", None),
    )
    body = functools.partial(shards, mesh.shape["seq"], mesh.shape["dp"])
    return jax.shard_map(body, mesh=mesh, in_specs=in_specs, out_specs=out_specs, check_vma=False)
```

time: 198 us -> 88.9 us (0.45)
  Pallas kernels: 0 us -> 80.2 us
  waiting for transfers between devices: 50.1 us -> 0 us
  matrix products: 35.2 us -> 0 us
  local copies, waits for them, and re-layouts: 37.6 us -> 6.52 us
  blocking collectives: 25.1 us -> 0 us
  other arithmetic: 17.6 us -> 0 us
  starting transfers between devices: 17.2 us -> 0 us
  between operations: 14 us -> 0.67 us
    pallas_call x0 -> x1, Pallas kernels: none -> 80.2 us  [shards(): pl.pallas_call(functools.partial(kernel, n_seq, n_dp), out_shape=(jax.Sha...]
    all_to_all x3 -> x0, waiting for transfers between devices: 49.4 us -> none  [the longest x1 18 us: shards(): lax.all_to_all(mixed_one, 'seq', split_axis=1, concat_axis=0, tiled=True)]
    dot_general x9 -> x0, matrix products: 35.2 us -> none  [the longest x1 11.6 us: shards(): jnp.einsum('tnh,nch->tnc', grad_pre, up_back, preferred_element_type=jnp....]
    all_to_all x1 -> x0, blocking collectives: 25.1 us -> none  [shards(): lax.all_to_all(grad_two, 'seq', split_axis=1, concat_axis=0, tiled=True)]
    all_to_all x3 -> x0, starting transfers between devices: 17.1 us -> none  [the longest x1 8.44 us: shards(): lax.all_to_all(mixed_one, 'seq', split_axis=1, concat_axis=0, tiled=True)]
    convert_element_type x8 -> x0, local copies, waits for them, and re-layouts: 16.1 us -> none  [the longest x3 8.84 us: shards(): mixed_f = mixed_two.reshape(tok_rows, channels).astype(jnp.float32)]
    unnamed x2 -> x0, other arithmetic: 12 us -> none
    unnamed x32 -> x9, local copies, waits for them, and re-layouts: 18.4 us -> 6.51 us
  transfers between devices with their start and end apart: 7 -> 0, of which waited for: 3 -> 0; matrix products, arithmetic and copies ran while one was open for 29% -> 0% of each run, Pallas kernels for 0% -> 0%
where the time goes in v1:
time: 88.9 us; the launch traced here: 87.4 us
  Pallas kernels  80.2 us (90%)
  local copies, waits for them, and re-layouts  6.52 us (7%)
    pallas_call x1, Pallas kernels, shards(): pl.pallas_call(functools.partial(kernel, n_seq, n_dp), out_shape=(jax.Sha...  80.2 us
    unnamed x9, local copies, waits for them, and re-layouts  6.51 us

profile of v1, /device:TPU:0, one launch (start us, length us, event | category | flops | bytes accessed | tf_op | source)
XLA Modules:
  0.0 87.4 jit_solution(13041161935015886969)
XLA Ops:
  0.6 1.0 %copy.10 = bf16[32,16,16]{2,1,0:T(8,128)(2,1)S(1)} copy(bf16[32,16,16]{0,2,1:T(8,128)(2,1)} %param.9) | data formatting | bytes 32768 | tf_op args[3]
  1.6 0.0 copy-start
  1.6 1.0 %copy-done = bf16[1,512,512]{2,1,0:T(8,128)(2,1)S(1)} copy-done((bf16[1,512,512]{2,1,0:T(8,128)(2,1)S(1)}, bf16[1,512,512]{2,1,0:T(8,128)(2,1)}, u32[]{:S(2)}) %copy-start) | copy-done | bytes 524312
  2.7 80.2 %shard_map.93 = (bf16[512,768]{1,0:T(8,128)(2,1)}, bf16[512,768]{1,0:T(8,128)(2,1)}, f32[256,512]{1,0:T(8,128)S(1)}, f32[256,128]{1,0:T(8,128)S(1)}) custom-call(bf16[512,768]{1,0:T(8,128)(2,1)} %bitcast.14, bf16[512,768]{1,0:T(8,128)(2,1)} %bitcast.15, bf16[512,512]{1,0:T(8,128)(2,1)S(1)} %bitcast.11, bf16[512,16]{1,0:T(8,128)(2,1)S(1)} %bitcast.10, ...), custom_call_target="tpu_custom_call" | custom-call | flops 7247757312 | bytes 8388608 | tf_op jit(solution)/shard_map/pallas_call | solution.py:288
  82.9 0.0 copy-start.1
  82.9 0.7 copy.11
  83.7 2.1 %copy.15 = bf16[1,512,768]{2,1,0:T(8,128)(2,1)} copy(bf16[1,512,768]{2,1,0:T(8,128)(2,1)} %bitcast.13) | data formatting | bytes 1572864
  85.7 0.0 copy-done.1
  85.7 0.9 %copy.16 = bf16[1,512,768]{2,1,0:T(8,128)(2,1)} copy(bf16[1,512,768]{2,1,0:T(8,128)(2,1)S(1)} %bitcast.12) | data formatting | bytes 1572864
  86.6 0.8 copy.17
  (1 shorter events, 0.0 us)
Async XLA Ops:
  1.6 1.0 %copy-start = (bf16[1,512,512]{2,1,0:T(8,128)(2,1)S(1)}, bf16[1,512,512]{2,1,0:T(8,128)(2,1)}, u32[]{:S(2)}) copy-start(bf16[1,512,512]{2,1,0:T(8,128)(2,1)} %param.8) | copy-start | bytes 1572868
  82.9 2.8 %copy-start.1 = (bf16[512,768]{1,0:T(8,128)(2,1)S(1)}, bf16[512,768]{1,0:T(8,128)(2,1)}, u32[]{:S(2)}) copy-start(bf16[512,768]{1,0:T(8,128)(2,1)} %get-tuple-element.9) | copy-start | bytes 2359300

commit v2 on v1

--- a/solution.py
+++ b/solution.py
@@ -26,10 +26,10 @@
 
 def kernel(
     n_seq, n_dp,
-    x_ref, cot_ref, f1_ref, f2_ref, up_ref, down_ref,
+    x_in, cot_in, f1_in, f2_ref, up_ref, down_ref,
     out_ref, gin_ref, g1_ref, g2_ref,
-    src, dst, up_all, down_all, mix, mix_t, f1_t, sel, perm, gate, t1, t1_in, t2, t2_in,
-    send_sem, recv_sem, w_send, w_recv, w_local, r_send, r_recv,
+    x_ref, cot_ref, f1_ref, src, dst, up_all, down_all, mix, mix_t, f1_t, gate, t1, t1_in, t2, t2_in,
+    send_sem, recv_sem, w_send, w_recv, w_local, in_sem, r_send, r_recv,
 ):
     me = lax.axis_index("seq")
     core = lax.axis_index("dp")
@@ -37,6 +37,13 @@
     groups, _, parts, width = src.shape[1], src.shape[2], src.shape[3], src.shape[4]
     rows_one = t1_in.shape[1]
     rows_two = t2_in.shape[1]
+    loads = [
+        pltpu.make_async_copy(x_in, x_ref, in_sem.at[0]),
+        pltpu.make_async_copy(f1_in, f1_ref, in_sem.at[1]),
+        pltpu.make_async_copy(cot_in, cot_ref, in_sem.at[2]),
+    ]
+    loads[0].start()
+    loads[1].start()
 
     barrier = pltpu.get_barrier_semaphore()
 
@@ -63,7 +70,9 @@
 
     def send(phase, g):
         def one(k, carry):
-            peer = lax.rem(me + k, n_seq)
+            step = (k + 1) // 2
+            shift = n_seq // 2 + jnp.where(k % 2 == 1, step, -step)
+            peer = lax.rem(me + shift, n_seq)
             pltpu.make_async_remote_copy(
                 src_ref=src.at[phase, g, peer],
                 dst_ref=dst.at[phase, g, me],
@@ -74,7 +83,7 @@
             ).start()
             return carry
 
-        lax.fori_loop(1, n_seq, one, 0)
+        lax.fori_loop(0, n_seq - 1, one, 0)
         dst[phase, g, me] = src[phase, g, me]
 
     def receive(phase, g):
@@ -100,6 +109,8 @@
 
         lax.fori_loop(0, n_seq // seq_tile, step, 0)
 
+    loads[0].wait()
+    loads[1].wait()
     mul_into(0, 0, f1_ref, lambda: x_ref[:, cols(0)])
     pl.semaphore_wait(barrier, n_seq + n_dp - 2)
     send(0, 0)
@@ -122,7 +133,7 @@
         pltpu.make_async_copy(up_ref, up_all.at[core], w_local.at[0]),
         pltpu.make_async_copy(down_ref, down_all.at[core], w_local.at[1]),
     ]
-    for copy in own:
+    for copy in own + loads[2:]:
         copy.start()
     for g in range(1, groups):
         mul_into(0, g, f1_ref, lambda: x_ref[:, cols(g)])
@@ -131,22 +142,19 @@
     def iota(shape, axis):
         return lax.broadcasted_iota(jnp.int32, shape, axis)
 
-    square = (block, block)
-    per = n_seq // n_dp
-    a_row, a_col = iota((n_seq, block), 0), iota((n_seq, block), 1)
-    spread = jnp.where(a_row == a_col // parts, 1.0, 0.0).astype(BF16)
-    k_row, k_col = iota((block, 128), 0), iota((block, 128), 1)
-    sel[...] = jnp.where(k_row // parts == k_col, 1.0, 0.0).astype(BF16)
-    row, col = iota(square, 0), iota(square, 1)
-    to_q = (row // (parts * per)) * per + row % per
-    to_p = (row // per) % parts
-    perm[...] = jnp.where(col == to_q * parts + to_p, 1.0, 0.0).astype(BF16)
-    order = jnp.where(col == (row % parts) * n_seq + row // parts, 1.0, 0.0).astype(BF16)
-    wide = dot(f2_ref[...], spread).astype(BF16)
-    full = dot(order, wide)
-    full = jnp.where(row % parts == col % parts, full, 0.0)
-    mix[...] = full.astype(BF16)
-    mix_t[...] = full.T.astype(BF16)
+    tiles = jnp.where(iota((parts, block), 0) == iota((parts, block), 1) % parts, 1.0, 0.0)
+    tiles_low = tiles.astype(BF16)
+    own_a = iota((n_seq, block), 0) == iota((n_seq, block), 1) // parts
+
+    def build(q, carry):
+        wide = dot(f2_ref[pl.ds(pl.multiple_of(q * n_seq, n_seq), n_seq), :], tiles_low)
+        line = jnp.sum(jnp.where(own_a, wide, 0.0), axis=0, keepdims=True)
+        t1[pl.ds(pl.multiple_of(q * parts, parts), parts), :] = tiles * line
+        return carry
+
+    lax.fori_loop(0, n_seq, build, 0)
+    mix[...] = t1[...].astype(BF16)
+    mix_t[...] = t1[...].T.astype(BF16)
     f1_t[...] = f1_ref[...].astype(F32).T.astype(BF16)
 
     for g in range(groups):
@@ -154,7 +162,7 @@
         mul_into(1, g, mix, lambda: flat(dst, 0, g))
         send(1, g)
 
-    for copy in own:
+    for copy in own + loads[2:]:
         copy.wait()
     for i, everyone in enumerate((up_all, down_all)):
         span = everyone.at[pl.ds(0, n_dp - 1)]
@@ -206,23 +214,16 @@
         mul_into(3, g, mix_t, lambda: flat(dst, 2, g))
         send(3, g)
 
-    def term_two(rows):
+    same = iota((parts, block), 0) == iota((parts, block), 1) % parts
+    for tile in range(0, n_seq, seq_tile):
+        rows = pl.ds(tile, seq_tile)
         total = None
         for g in range(groups):
-            grads = dot(perm[rows, :], flat(dst, 2, g)).astype(BF16)
+            grads = dst[2, g, rows].reshape(seq_tile * parts, width)
             part = dot_nt(grads, flat(dst, 0, g))
             total = part if total is None else total + part
-        start = rows.start
-        r = start + iota(total.shape, 0)
-        c = iota(total.shape, 1)
-        total = jnp.where((r // per) % parts == c % parts, total, 0.0)
-        high = total.astype(BF16)
-        rest = total - high.astype(F32)
-        low = rest.astype(BF16)
-        last = (rest - low.astype(F32)).astype(BF16)
-        t2[rows, :] = dot(high, sel[...]) + dot(low, sel[...]) + dot(last, sel[...])
-
-    row_loop(block, ROW_TILE, term_two)
+        total = jnp.where(same[None], total.reshape(seq_tile, parts, block), 0.0)
+        t2[rows, :] = jnp.sum(total, axis=1)
 
     def reduce_start(which, whole, landed, size):
         def one(k, carry):
@@ -275,27 +276,44 @@
             pltpu.make_async_copy(span, span, send_sem.at[phase, g]).wait()
 
 
+def finish(out_ref, gin_ref, g1_ref, g2_ref, out, gin, g1, g2, sem):
+    copies = [
+        pltpu.make_async_copy(a, b, sem.at[i])
+        for i, (a, b) in enumerate(((out_ref, out), (gin_ref, gin), (g1_ref, g1)))
+    ]
+    for copy in copies:
+        copy.start()
+    _, n_a, parts = g2.shape
+    for a in range(n_a):
+        g2[:, a, :] = g2_ref[:, a * parts:(a + 1) * parts]
+    for copy in copies:
+        copy.wait()
+
+
 def shards(n_seq, n_dp, inputs, cotangent, factor_one, factor_two, up_weight, down_weight):
     _, block, channels = inputs.shape
     groups, width, hid = up_weight.shape
     parts = block // n_seq
     per = n_seq // n_dp
     vmem = pl.BlockSpec(memory_space=pltpu.VMEM)
-    anywhere = pl.BlockSpec(memory_space=pl.ANY)
-    rows_one, rows_two = block // n_dp, parts * per
+    hbm = pl.BlockSpec(memory_space=pltpu.HBM)
+    rows_one, rows_two = block // n_dp, per
     exchange = pltpu.VMEM((4, groups, n_seq, parts, width), BF16)
     flops = 2 * block * block * channels * 6 + 2 * block * width * hid * n_dp * groups * 4
     out, gin, g1, g2 = pl.pallas_call(
         functools.partial(kernel, n_seq, n_dp),
         out_shape=(
-            jax.ShapeDtypeStruct((block, channels), BF16),
-            jax.ShapeDtypeStruct((block, channels), BF16),
-            jax.ShapeDtypeStruct((rows_one, block), F32),
-            jax.ShapeDtypeStruct((rows_two, 128), F32),
+            pltpu.VMEM((block, channels), BF16),
+            pltpu.VMEM((block, channels), BF16),
+            pltpu.VMEM((rows_one, block), F32),
+            pltpu.VMEM((rows_two, block), F32),
         ),
-        in_specs=[vmem, vmem, vmem, vmem, anywhere, anywhere],
+        in_specs=[hbm, hbm, hbm, vmem, hbm, hbm],
         out_specs=(vmem, vmem, vmem, vmem),
         scratch_shapes=[
+            pltpu.VMEM((block, channels), BF16),
+            pltpu.VMEM((block, channels), BF16),
+            pltpu.VMEM((block, block), BF16),
             exchange,
             exchange,
             pltpu.VMEM((n_dp, groups, width, hid), BF16),
@@ -303,30 +321,42 @@
             pltpu.VMEM((block, block), BF16),
             pltpu.VMEM((block, block), BF16),
             pltpu.VMEM((block, block), BF16),
-            pltpu.VMEM((block, 128), BF16),
-            pltpu.VMEM((block, block), BF16),
             pltpu.VMEM((block, channels), F32),
             pltpu.VMEM((block, block), F32),
             pltpu.VMEM((n_dp, rows_one, block), F32),
-            pltpu.VMEM((block, 128), F32),
-            pltpu.VMEM((n_dp, rows_two, 128), F32),
+            pltpu.VMEM((n_seq, block), F32),
+            pltpu.VMEM((n_dp, rows_two, block), F32),
             pltpu.SemaphoreType.DMA((4, groups)),
             pltpu.SemaphoreType.DMA((4, groups)),
             pltpu.SemaphoreType.DMA((2,)),
             pltpu.SemaphoreType.DMA((2,)),
             pltpu.SemaphoreType.DMA((2,)),
+            pltpu.SemaphoreType.DMA((3,)),
             pltpu.SemaphoreType.DMA((2,)),
             pltpu.SemaphoreType.DMA((2,)),
         ],
         compiler_params=pltpu.CompilerParams(
-            collective_id=0, has_side_effects=True, vmem_limit_bytes=52 * 2**20
+            collective_id=0, has_side_effects=True, vmem_limit_bytes=58 * 2**20
         ),
         cost_estimate=pl.CostEstimate(flops=flops, bytes_accessed=2**23, transcendentals=2**21),
     )(
         inputs[0], cotangent[0], factor_one[0],
-        factor_two.reshape(block, n_seq), up_weight, down_weight,
+        factor_two.transpose(1, 2, 0).reshape(n_seq * n_seq, parts), up_weight, down_weight,
     )
-    return out[None], gin[None], g1[None], g2[:, :n_seq].reshape(parts, per, n_seq)
+    out, gin, g1, g2 = pl.pallas_call(
+        finish,
+        out_shape=(
+            jax.ShapeDtypeStruct((block, channels), BF16),
+            jax.ShapeDtypeStruct((block, channels), BF16),
+            jax.ShapeDtypeStruct((rows_one, block), F32),
+            jax.ShapeDtypeStruct((per, n_seq, parts), F32),
+        ),
+        in_specs=[vmem, vmem, vmem, vmem],
+        out_specs=(hbm, hbm, hbm, vmem),
+        scratch_shapes=[pltpu.SemaphoreType.DMA((3,))],
+        compiler_params=pltpu.CompilerParams(vmem_limit_bytes=8 * 2**20),
+    )(out, gin, g1, g2)
+    return out[None], gin[None], g1[None], g2.transpose(2, 0, 1)
 
 
 def solution(mesh):

time: 88.9 us -> 82.6 us (0.929)
  local copies, waits for them, and re-layouts: 6.52 us -> 0 us
  Pallas kernels: 80.2 us -> 81.1 us
    unnamed x9 -> x0, local copies, waits for them, and re-layouts: 6.51 us -> none
    pallas_call x1 -> x2, Pallas kernels: 80.2 us -> 81.1 us  [the longest x1 79.1 us: shards(): pl.pallas_call(functools.partial(kernel, n_seq, n_dp), out_shape=(pltpu.V...]
where the time goes in v2:
time: 82.6 us; the launch traced here: 81.7 us
  Pallas kernels  81.1 us (98%)
    pallas_call x1, Pallas kernels, shards(): pl.pallas_call(functools.partial(kernel, n_seq, n_dp), out_shape=(pltpu.V...  79.1 us
    pallas_call x1, Pallas kernels, shards(): pl.pallas_call(finish, out_shape=(jax.ShapeDtypeStruct((block, channels),...  1.97 us

profile of v2, /device:TPU:0, one launch (start us, length us, event | category | flops | bytes accessed | tf_op | source)
XLA Modules:
  0.0 81.7 jit_solution(2622219164245829849)
XLA Ops:
  0.6 79.1 %shard_map.93 = (bf16[512,768]{1,0:T(8,128)(2,1)S(1)}, bf16[512,768]{1,0:T(8,128)(2,1)S(1)}, f32[256,512]{1,0:T(8,128)S(1)}, f32[8,512]{1,0:T(8,128)S(1)}) custom-call(bf16[512,768]{1,0:T(8,128)(2,1)} %bitcast.10, bf16[512,768]{1,0:T(8,128)(2,1)} %bitcast.11, bf16[512,512]{1,0:T(8,128)(2,1)} %bitcast.14, bf16[256,32]{1,0:T(8,128)(2,1)} %bitcast.16, ...), custom_call_target="tpu_custom_call" | custom-call | flops 7247757312 | bytes 8388608 | tf_op jit(solution)/shard_map/pallas_call | solution.py:303
  79.8 2.0 %shard_map.94 = (bf16[512,768]{1,0:T(8,128)(2,1)}, bf16[512,768]{1,0:T(8,128)(2,1)}, f32[256,512]{1,0:T(8,128)}, f32[8,16,32]{2,1,0:T(8,128)}) custom-call(bf16[512,768]{1,0:T(8,128)(2,1)S(1)} %get-tuple-element.12.out_ref, bf16[512,768]{1,0:T(8,128)(2,1)S(1)} %get-tuple-element.13.gin_ref, f32[256,512]{1,0:T(8,128)S(1)} %get-tuple-element.14.g1_ref, ...), custom_call_target="tpu_custom_call" | custom-call | tf_op jit(solution)/shard_map/pallas_call | solution.py:346

commit v3 on v2

--- a/solution.py
+++ b/solution.py
@@ -28,15 +28,16 @@
     n_seq, n_dp,
     x_in, cot_in, f1_in, f2_ref, up_ref, down_ref,
     out_ref, gin_ref, g1_ref, g2_ref,
-    x_ref, cot_ref, f1_ref, src, dst, up_all, down_all, mix, mix_t, f1_t, gate, t1, t1_in, t2, t2_in,
+    x_ref, cot_ref, f1_ref, src, dst, up_all, down_all, mix, mix_t, f1_t, gate, t1, x_all, g_all, t2, t2_in,
     send_sem, recv_sem, w_send, w_recv, w_local, in_sem, r_send, r_recv,
 ):
     me = lax.axis_index("seq")
     core = lax.axis_index("dp")
     block, channels = x_ref.shape
     groups, _, parts, width = src.shape[1], src.shape[2], src.shape[3], src.shape[4]
-    rows_one = t1_in.shape[1]
+    rows_one = g1_ref.shape[0]
     rows_two = t2_in.shape[1]
+    per = n_seq // n_dp
     loads = [
         pltpu.make_async_copy(x_in, x_ref, in_sem.at[0]),
         pltpu.make_async_copy(f1_in, f1_ref, in_sem.at[1]),
@@ -126,6 +127,14 @@
                 device_id={"dp": peer},
                 device_id_type=MESH,
             ).start()
+        pltpu.make_async_remote_copy(
+            src_ref=x_ref,
+            dst_ref=x_all.at[core],
+            send_sem=r_send.at[0],
+            recv_sem=r_recv.at[0],
+            device_id={"dp": peer},
+            device_id_type=MESH,
+        ).start()
         return carry
 
     lax.fori_loop(1, n_dp, send_weights, 0)
@@ -253,20 +262,45 @@
 
     reduce_start(1, t2, t2_in, rows_two)
 
+    reduce_end(1, t2, t2_in, rows_two, g2_ref)
+    others = x_all.at[pl.ds(0, n_dp - 1)]
+    pltpu.make_async_copy(others, others, r_recv.at[0]).wait()
+
+    def forward(g):
+        def one(k, carry):
+            peer = lax.rem(core + k, n_dp)
+            pltpu.make_async_remote_copy(
+                src_ref=dst.at[3, g, pl.ds(peer * per, per)],
+                dst_ref=g_all.at[g, core],
+                send_sem=r_send.at[2 + g],
+                recv_sem=r_recv.at[2 + g],
+                device_id={"dp": peer},
+                device_id_type=MESH,
+            ).start()
+            return carry
+
+        lax.fori_loop(1, n_dp, one, 0)
+
     for g in range(groups):
         receive(3, g)
-        grads = flat(dst, 3, g)
-        seqs = x_ref[:, cols(g)]
+        forward(g)
+        gin_ref[:, cols(g)] = (gate[:, cols(g)] + dot(f1_t[...], flat(dst, 3, g))).astype(BF16)
+        mine = dst[3, g, pl.ds(core * per, per)].reshape(rows_one, width)
+        part = dot_nt(mine, x_ref[:, cols(g)])
         if g == 0:
-            t1[...] = dot_nt(grads, seqs)
+            g1_ref[...] = part
         else:
-            t1[...] += dot_nt(grads, seqs)
-        if g == groups - 1:
-            reduce_start(0, t1, t1_in, rows_one)
-        gin_ref[:, cols(g)] = (gate[:, cols(g)] + dot(f1_t[...], grads)).astype(BF16)
-
-    reduce_end(1, t2, t2_in, rows_two, g2_ref)
-    reduce_end(0, t1, t1_in, rows_one, g1_ref)
+            g1_ref[...] += part
+        span = g_all.at[g, pl.ds(0, n_dp - 1)]
+        pltpu.make_async_copy(span, span, r_recv.at[2 + g]).wait()
+        for k in range(1, n_dp):
+            d = lax.rem(core + k, n_dp)
+            g1_ref[...] += dot_nt(g_all[g, d].reshape(rows_one, width), x_all[d, :, cols(g)])
+
+    pltpu.make_async_copy(others, others, r_send.at[0]).wait()
+    for g in range(groups):
+        span = g_all.at[g, pl.ds(0, n_dp - 1)]
+        pltpu.make_async_copy(span, span, r_send.at[2 + g]).wait()
     for i, everyone in enumerate((up_all, down_all)):
         span = everyone.at[pl.ds(0, n_dp - 1)]
         pltpu.make_async_copy(span, span, w_send.at[i]).wait()
@@ -323,7 +357,8 @@
             pltpu.VMEM((block, block), BF16),
             pltpu.VMEM((block, channels), F32),
             pltpu.VMEM((block, block), F32),
-            pltpu.VMEM((n_dp, rows_one, block), F32),
+            pltpu.VMEM((n_dp, block, channels), BF16),
+            pltpu.VMEM((groups, n_dp, per, parts, width), BF16),
             pltpu.VMEM((n_seq, block), F32),
             pltpu.VMEM((n_dp, rows_two, block), F32),
             pltpu.SemaphoreType.DMA((4, groups)),
@@ -332,8 +367,8 @@
             pltpu.SemaphoreType.DMA((2,)),
             pltpu.SemaphoreType.DMA((2,)),
             pltpu.SemaphoreType.DMA((3,)),
-            pltpu.SemaphoreType.DMA((2,)),
-            pltpu.SemaphoreType.DMA((2,)),
+            pltpu.SemaphoreType.DMA((2 + groups,)),
+            pltpu.SemaphoreType.DMA((2 + groups,)),
         ],
         compiler_params=pltpu.CompilerParams(
             collective_id=0, has_side_effects=True, vmem_limit_bytes=58 * 2**20

time: 82.6 us -> 82 us (level)
  no operation moved by 1% of the time
where the time goes in v3:
time: 82 us; the launch traced here: 81 us
  Pallas kernels  80.4 us (98%)
    pallas_call x1, Pallas kernels, shards(): pl.pallas_call(functools.partial(kernel, n_seq, n_dp), out_shape=(pltpu.V...  78.4 us
    pallas_call x1, Pallas kernels, shards(): pl.pallas_call(finish, out_shape=(jax.ShapeDtypeStruct((block, channels),...  1.97 us

profile of v3, /device:TPU:0, one launch (start us, length us, event | category | flops | bytes accessed | tf_op | source)
XLA Modules:
  0.0 81.0 jit_solution(580691256368169115)
XLA Ops:
  0.6 78.4 %shard_map.93 = (bf16[512,768]{1,0:T(8,128)(2,1)S(1)}, bf16[512,768]{1,0:T(8,128)(2,1)S(1)}, f32[256,512]{1,0:T(8,128)S(1)}, f32[8,512]{1,0:T(8,128)S(1)}) custom-call(bf16[512,768]{1,0:T(8,128)(2,1)} %bitcast.10, bf16[512,768]{1,0:T(8,128)(2,1)} %bitcast.11, bf16[512,512]{1,0:T(8,128)(2,1)} %bitcast.14, bf16[256,32]{1,0:T(8,128)(2,1)} %bitcast.16, ...), custom_call_target="tpu_custom_call" | custom-call | flops 7247757312 | bytes 8388608 | tf_op jit(solution)/shard_map/pallas_call | solution.py:337
  79.1 2.0 %shard_map.94 = (bf16[512,768]{1,0:T(8,128)(2,1)}, bf16[512,768]{1,0:T(8,128)(2,1)}, f32[256,512]{1,0:T(8,128)}, f32[8,16,32]{2,1,0:T(8,128)}) custom-call(bf16[512,768]{1,0:T(8,128)(2,1)S(1)} %get-tuple-element.12.out_ref, bf16[512,768]{1,0:T(8,128)(2,1)S(1)} %get-tuple-element.13.gin_ref, f32[256,512]{1,0:T(8,128)S(1)} %get-tuple-element.14.g1_ref, ...), custom_call_target="tpu_custom_call" | custom-call | tf_op jit(solution)/shard_map/pallas_call | solution.py:381
